TPU v7x, 256 devices: a whole 4x4x8 slice. The times are simulated.
256 devices in a mesh: group: 16 (over y, z_hi), space: 16 (over x, z_lo, core).
Axes of the slice: x: 4, y: 4, z: 8 (z_hi: 4, z_lo: 2; z = z_hi * 2 + z_lo), core: 2. Of those that a mesh axis runs over, the one named last changes fastest.
Arguments:
- factors: bfloat16 [16, 96, 524288], P('group', None, 'space'), may hold values from -30 to 30
Outputs:
- merged: bfloat16 [16, 96, 524288], P('group', None, 'space')
- energy: float32 [16, 96, 96], P('group')
All inputs are finite; a program needn't handle non-finite values.
Results may differ from a plain program's by a relative error of at most 0.033.
Values may be sent and summed in bfloat16 or wider, within the bound.
No kernel may reach another device: no remote copies, remote signals or barrier semaphores. Data moves between devices by JAX's collectives and lax.ppermute only.
A program may use at most 128 MiB of HBM per device.

v0:
```python
import jax
import jax.numpy as jnp
from jax import lax
from jax.sharding import PartitionSpec as P

ITERS = 4


def partner(x, axis, distance):
    return lax.ppermute(x, axis, [(i, i ^ 1 << distance) for i in range(lax.axis_size(axis))])


def gram_block(left, right):
    return lax.dot_general(
        left, right, (((1,), (1,)), ((), ())), preferred_element_type=jnp.float32
    )


def orthogonal_iteration(own_block, cross_block, other_block, is_low, row_total):
    rank = own_block.shape[0]
    top_left = jnp.where(is_low, own_block, other_block)
    bottom_right = jnp.where(is_low, other_block, own_block)
    top_right = jnp.where(is_low, cross_block, cross_block.T)
    whole_gram = jnp.concatenate(
        [
            jnp.concatenate([top_left, top_right], axis=1),
            jnp.concatenate([top_right.T, bottom_right], axis=1),
        ],
        axis=0,
    )
    subspace = jnp.eye(2 * rank, rank, dtype=jnp.float32)
    for turn_index in range(ITERS):
        image = jnp.dot(whole_gram, subspace, precision=lax.Precision.HIGHEST)
        inner = jnp.dot(image.T, image, precision=lax.Precision.HIGHEST)
        lower_factor = jnp.linalg.cholesky(inner)
        subspace = jax.scipy.linalg.solve_triangular(lower_factor, image.T, lower=True).T
    energy = (
        jnp.dot(
            subspace.T,
            jnp.dot(whole_gram, subspace, precision=lax.Precision.HIGHEST),
            precision=lax.Precision.HIGHEST,
        )
        / row_total
    )
    upper_rows = subspace[:rank]
    lower_rows = subspace[rank:]
    coef_mine = jnp.where(is_low, upper_rows, lower_rows).astype(jnp.bfloat16)
    coef_other = jnp.where(is_low, lower_rows, upper_rows).astype(jnp.bfloat16)
    return (coef_mine, coef_other, energy)


def combine(coef_mine, own_rows, coef_other, other_rows):
    dims = (((0,), (0,)), ((), ()))
    total = lax.dot_general(coef_mine, own_rows, dims, preferred_element_type=jnp.float32)
    total = total + lax.dot_general(
        coef_other, other_rows, dims, preferred_element_type=jnp.float32
    )
    return total.astype(jnp.bfloat16)


def local(factors):
    own_factor = factors[0]
    row_local = own_factor.shape[1]
    row_total = row_local * lax.axis_size("space")
    group_index = lax.axis_index("group")
    energy = None
    for section_bit in (0, 1):
        is_low = group_index // (1 << section_bit) % 2 == 0
        partner_factor = partner(own_factor, "group", section_bit)
        own_block, cross_block, other_block = lax.psum(
            (
                gram_block(own_factor, own_factor),
                gram_block(own_factor, partner_factor),
                gram_block(partner_factor, partner_factor),
            ),
            "space",
        )
        coef_mine, coef_other, energy = orthogonal_iteration(
            own_block, cross_block, other_block, is_low, row_total
        )
        own_factor = combine(coef_mine, own_factor, coef_other, partner_factor)
    return (own_factor[None], energy[None])


def solution(mesh):
    return jax.shard_map(
        local,
        mesh=mesh,
        in_specs=(P("group", None, "space"),),
        out_specs=(P("group", None, "space"), P("group", None, None)),
        check_vma=False,
    )
```

profile of v0, /device:TPU:33, one launch (start us, length us, event | category | flops | bytes accessed | tf_op | source)
XLA Modules:
  0.0 990.9 jit_solution(3733030128906096281)
XLA Ops:
  10.3 7.2 fusion.68
  17.5 262.7 %collective-permute-done = bf16[96,32768]{1,0:T(8,128)(2,1)S(1)} collective-permute-done((bf16[96,32768]{1,0:T(8,128)(2,1)}, bf16[96,32768]{1,0:T(8,128)(2,1)S(1)}, u32[]{:S(2)}, u32[]{:S(2)}) %collective-permute-start) | collective-permute-done | bytes 6291488 | tf_op jit(solution)/shard_map/ppermute | solution.py:10
  285.6 113.5 %all-reduce.7.cloned.1.call-done = (f32[96,96]{1,0:T(8,128)}, f32[96,96]{1,0:T(8,128)}, f32[96,96]{0,1:T(8,128)}) async-done(((f32[96,96]{1,0:T(8,128)}, f32[96,96]{1,0:T(8,128)}, f32[96,96]{0,1:T(8,128)}), (f32[96,96]{1,0:T(8,128)}, f32[96,96]{1,0:T(8,128)}, f32[96,96]{0,1:T(8,128)})) %all-reduce.7.cloned.1.call-update) | async-done | bytes 110608 | tf_op jit(solution)/shard_map/psum | solution.py:70
  401.7 8.8 cholesky.134
  411.8 7.4 custom-call.12
  420.4 8.8 cholesky.145
  430.5 7.4 custom-call.13
  439.1 8.8 cholesky.156
  449.2 7.5 custom-call.14
  458.0 8.8 cholesky.167
  468.1 7.4 custom-call.15
  475.7 9.3 fusion.59
  500.1 250.7 %collective-permute-done.1 = bf16[96,32768]{1,0:T(8,128)(2,1)S(1)} collective-permute-done((bf16[96,32768]{1,0:T(8,128)(2,1)S(1)}, bf16[96,32768]{1,0:T(8,128)(2,1)S(1)}, u32[]{:S(2)}, u32[]{:S(2)}) %collective-permute-start.1) | collective-permute-done | bytes 6291488 | tf_op jit(solution)/shard_map/ppermute | solution.py:10
  755.9 130.6 %all-reduce.5.cloned.1.call-done = (f32[96,96]{1,0:T(8,128)}, f32[96,96]{1,0:T(8,128)}, f32[96,96]{0,1:T(8,128)}) async-done(((f32[96,96]{1,0:T(8,128)}, f32[96,96]{1,0:T(8,128)}, f32[96,96]{0,1:T(8,128)}), (f32[96,96]{1,0:T(8,128)}, f32[96,96]{1,0:T(8,128)}, f32[96,96]{0,1:T(8,128)})) %all-reduce.5.cloned.1.call-update) | async-done | bytes 110608 | tf_op jit(solution)/shard_map/psum | solution.py:70
  889.9 8.8 cholesky.178
  900.0 7.4 custom-call.16
  908.6 8.8 cholesky.189
  918.8 7.5 custom-call.17
  927.5 8.8 cholesky.200
  937.6 7.4 custom-call.18
  946.2 8.8 cholesky.211
  956.3 7.4 custom-call.19
  965.4 9.3 fusion.60
  974.7 9.1 fusion.2
  (104 shorter events, 54.2 us)
Async XLA Ops:
  7.2 391.9 %all-reduce.7.cloned.1.call-start = ((), (), s32[]{:S(2)}) async-start(), calls=%async_computation.1 | async-start | bytes 294912 | tf_op jit(solution)/shard_map/psum | solution.py:70
  7.2 273.0 %copy-start.3 = (bf16[1,96,32768]{2,1,0:T(8,128)(2,1)S(1)}, bf16[1,96,32768]{2,1,0:T(8,128)(2,1)}, u32[]{:S(2)}) copy-start(bf16[1,96,32768]{2,1,0:T(8,128)(2,1)} %param.4) | copy-start | bytes 18874372
  7.2 273.0 %collective-permute-start = (bf16[96,32768]{1,0:T(8,128)(2,1)}, bf16[96,32768]{1,0:T(8,128)(2,1)S(1)}, u32[]{:S(2)}, u32[]{:S(2)}) collective-permute-start(bf16[96,32768]{1,0:T(8,128)(2,1)} %bitcast.157), channel_id=1, source_target_pairs={{0,16},{16,0},{32,48},{48,32},{64,80},{80,64},{96,112},{112,96},{1... | collective-permute-start | bytes 18874376 | tf_op jit(solution)/shard_map/ppermute | solution.py:10
  280.2 2.7 copy-start.2
  285.4 601.2 %all-reduce.5.cloned.1.call-start = ((), (), s32[]{:S(2)}) async-start(), calls=%async_computation | async-start | bytes 294912 | tf_op jit(solution)/shard_map/psum | solution.py:70
  458.0 27.1 %slice-start.2 = ((s8[6291456]{0:T(1024)(128)(4,1)}), s8[2097152]{0:T(1024)(128)(4,1)S(1)}, s32[]{:S(2)}) async-start(s8[6291456]{0:T(1024)(128)(4,1)} %bitcast.155), calls=%async_computation.4 | async-start | bytes 4194304
  475.7 9.4 slice-start.3
  491.5 259.3 %copy-start = (bf16[96,32768]{1,0:T(8,128)(2,1)}, bf16[96,32768]{1,0:T(8,128)(2,1)S(1)}, u32[]{:S(2)}) copy-start(bf16[96,32768]{1,0:T(8,128)(2,1)S(1)} %fusion) | copy-start | bytes 18874372
  491.5 259.3 %collective-permute-start.1 = (bf16[96,32768]{1,0:T(8,128)(2,1)S(1)}, bf16[96,32768]{1,0:T(8,128)(2,1)S(1)}, u32[]{:S(2)}, u32[]{:S(2)}) collective-permute-start(bf16[96,32768]{1,0:T(8,128)(2,1)S(1)} %fusion), channel_id=1, source_target_pairs={{0,32},{16,48},{32,0},{48,16},{64,96},{80,112},{96,64},{112,80},{1... | collective-permute-start | bytes 18874376 | tf_op jit(solution)/shard_map/ppermute | solution.py:10
  750.8 2.6 copy-start.1
  964.0 10.7 %slice-start = ((s8[6291456]{0:T(1024)(128)(4,1)}), s8[2097152]{0:T(1024)(128)(4,1)S(1)}, s32[]{:S(2)}) async-start(s8[6291456]{0:T(1024)(128)(4,1)} %bitcast.153), calls=%async_computation.2 | async-start | bytes 4194304
  965.4 9.4 slice-start.1
Sparse Core Ops, SparseCore 0:
  285.5 113.5 all-reduce.6
  756.0 130.4 all-reduce.4
where the time goes:
time: 998 us; the launch traced here: 991 us
  waiting for transfers between devices  758 us (76%)
  other arithmetic  143 us (14%)
  matrix products  63.7 us (6%)
  between operations  14.8 us (1%)
    ppermute x2, waiting for transfers between devices, partner(): lax.ppermute(x, axis, [(i, i ^ 1 << distance) for i in range(lax.axis_siz...  513 us
    psum x2, waiting for transfers between devices, local(): lax.psum((gram_block(own_factor, own_factor), gram_block(own_factor, part...  244 us
    another operation x24, other arithmetic, orthogonal_iteration(): lower_factor = jnp.linalg.cholesky(inner)  75.6 us
    another operation x16, other arithmetic, orthogonal_iteration(): jax.scipy.linalg.solve_triangular(lower_factor, image.T, lower=True)  64.4 us
  transfers between devices with their start and end apart: 4, of which 4 were waited for; matrix products, arithmetic and copies ran while one was open for 1% of the time, Pallas kernels for 0%

commit v1 on v0

v1 whole, which is shorter than its diff:
```python
import jax
import jax.numpy as jnp
from jax import lax
from jax.sharding import Mesh, PartitionSpec as P

ITERS = 4
HIGHEST = lax.Precision.HIGHEST


def pair_swap(x, axis):
    return lax.ppermute(x, axis, [(0, 1), (1, 0)])


def shifted(x, axis, step):
    n = lax.axis_size(axis)
    return lax.ppermute(x, axis, [(i, (i + step) % n) for i in range(n)])


def scatter_pair(x, axis):
    me = lax.axis_index(axis)
    low, high = jnp.split(x, 2, axis=0)
    keep = jnp.where(me == 0, low, high)
    give = jnp.where(me == 0, high, low)
    return keep + pair_swap(give, axis)


def gather_pair(x, axis):
    me = lax.axis_index(axis)
    other = pair_swap(x, axis)
    return jnp.concatenate([jnp.where(me == 0, x, other), jnp.where(me == 0, other, x)], axis=0)


def scatter_ring(x, axis):
    n = lax.axis_size(axis)
    me = lax.axis_index(axis)
    rows = x.shape[0] // n
    pieces = x.reshape(n, rows, x.shape[1])

    def piece(step):
        return lax.dynamic_index_in_dim(pieces, (me + step) % n, 0, keepdims=False)

    got = [shifted(piece(step), axis, step) for step in range(1, n)]
    return sum(got, piece(0))


def gather_ring(x, axis):
    n = lax.axis_size(axis)
    me = lax.axis_index(axis)
    got = [x] + [shifted(x, axis, step) for step in range(1, n)]
    stack = jnp.stack(got)
    order = (me - jnp.arange(n)) % n
    return stack[order].reshape(n * x.shape[0], x.shape[1])


def sum_ring(x, axis):
    n = lax.axis_size(axis)
    return sum([shifted(x, axis, step) for step in range(1, n)], x)


def sum_gram(gram):
    packed = jnp.concatenate(
        [gram[128 * i : 128 * i + 128, 128 * j : 128 * j + 128] for i in range(3) for j in range(i, 3)],
        axis=0,
    )
    part = scatter_pair(packed, "core")
    part = scatter_pair(part, "z_lo")
    part = scatter_ring(part, "x")
    part = sum_ring(part, "z_hi")
    part = gather_ring(part, "x")
    part = gather_pair(part, "z_lo")
    packed = gather_pair(part, "core").reshape(6, 128, 128)
    place = {}
    count = 0
    for i in range(3):
        for j in range(i, 3):
            place[i, j] = packed[count]
            if i != j:
                place[j, i] = packed[count].T
            count += 1
    return jnp.concatenate(
        [jnp.concatenate([place[i, j] for j in range(3)], axis=1) for i in range(3)], axis=0
    )


def orthogonal_iteration(whole_gram):
    rank = whole_gram.shape[0] // 2
    subspace = jnp.eye(2 * rank, rank, dtype=jnp.float32)
    for turn_index in range(ITERS):
        image = jnp.dot(whole_gram, subspace, precision=HIGHEST)
        inner = jnp.dot(image.T, image, precision=HIGHEST)
        lower_factor = jnp.linalg.cholesky(inner)
        subspace = jax.scipy.linalg.solve_triangular(lower_factor, image.T, lower=True).T
    return subspace


def solve(gram, row_total):
    half = gram.shape[0] // 2
    low = orthogonal_iteration(gram[:half, :half]).astype(jnp.bfloat16).astype(jnp.float32)
    high = orthogonal_iteration(gram[half:, half:]).astype(jnp.bfloat16).astype(jnp.float32)
    zero = jnp.zeros_like(low)
    first = jnp.concatenate(
        [jnp.concatenate([low, zero], axis=1), jnp.concatenate([zero, high], axis=1)], axis=0
    )
    second_gram = jnp.dot(first.T, jnp.dot(gram, first, precision=HIGHEST), precision=HIGHEST)
    subspace = orthogonal_iteration(second_gram)
    energy = (
        jnp.dot(subspace.T, jnp.dot(second_gram, subspace, precision=HIGHEST), precision=HIGHEST)
        / row_total
    )
    second = subspace.astype(jnp.bfloat16).astype(jnp.float32)
    return jnp.dot(first, second, precision=HIGHEST).astype(jnp.bfloat16), energy


def local(factors):
    own = factors[0]
    row_total = own.shape[1] * lax.axis_size(("x", "z_lo", "core"))
    rows = lax.all_to_all(own, "z_hi", 1, 0, tiled=True)
    gram = lax.dot_general(rows, rows, (((1,), (1,)), ((), ())), preferred_element_type=jnp.float32)
    coef, energy = solve(sum_gram(gram), row_total)
    merged = lax.dot_general(
        coef, rows, (((0,), (0,)), ((), ())), preferred_element_type=jnp.float32
    ).astype(jnp.bfloat16)
    merged = lax.all_gather(merged, "z_hi", axis=1, tiled=True)
    return (merged[None], energy[None])


def solution(mesh):
    fine = Mesh(mesh.devices.reshape(4, 4, 4, 2, 2), ("y", "z_hi", "x", "z_lo", "core"))
    group, space = ("y", "z_hi"), ("x", "z_lo", "core")
    return jax.shard_map(
        local,
        mesh=fine,
        in_specs=(P(group, None, space),),
        out_specs=(P(group, None, space), P(group, None, None)),
        check_vma=False,
    )
```

time: 998 us -> 597 us (0.60)
  waiting for transfers between devices: 758 us -> 276 us
  other arithmetic: 143 us -> 211 us
  matrix products: 63.7 us -> 28.8 us
  local copies, waits for them, and re-layouts: 2.77 us -> 27.9 us
  starting transfers between devices: 9.52 us -> 29.3 us
    ppermute x2 -> x13, waiting for transfers between devices: 513 us -> 18.8 us  [the longest x9 10.9 us: shifted(): return lax.ppermute(x, axis, [(i, (i + step) % n) for i in range(n)])]
    psum x2 -> x0, waiting for transfers between devices: 244 us -> none  [local(): lax.psum((gram_block(own_factor, own_factor), gram_block(own_factor, part...]
    all_to_all x0 -> x1, waiting for transfers between devices: none -> 140 us  [local(): rows = lax.all_to_all(own, 'z_hi', 1, 0, tiled=True)]
    all_gather x0 -> x1, waiting for transfers between devices: none -> 117 us  [local(): merged = lax.all_gather(merged, 'z_hi', axis=1, tiled=True)]
    another operation x24 -> x36, other arithmetic: 75.6 us -> 114 us  [orthogonal_iteration(): lower_factor = jnp.linalg.cholesky(inner)]
    dot_general x28 -> x31, matrix products: 61 us -> 24.7 us  [the longest x1 8.82 us: local(): lax.dot_general(rows, rows, (((1,), (1,)), ((), ())), preferred_element_t...]
    another operation x16 -> x24, other arithmetic: 64.4 us -> 96.3 us  [orthogonal_iteration(): jax.scipy.linalg.solve_triangular(lower_factor, image.T, lower=True)]
    all_to_all x0 -> x2, local copies, waits for them, and re-layouts: none -> 20.1 us  [local(): rows = lax.all_to_all(own, 'z_hi', 1, 0, tiled=True)]
  transfers between devices with their start and end apart: 4 -> 15, of which waited for: 4 -> 12; matrix products, arithmetic and copies ran while one was open for 1% -> 0% of each run, Pallas kernels for 0% -> 0%
where the time goes in v1:
time: 597 us; the launch traced here: 588 us
  waiting for transfers between devices  276 us (46%)
  other arithmetic  211 us (35%)
  starting transfers between devices  29.3 us (5%)
  matrix products  28.8 us (5%)
  local copies, waits for them, and re-layouts  27.9 us (5%)
  between operations  15 us (3%)
    all_to_all x1, waiting for transfers between devices, local(): rows = lax.all_to_all(own, 'z_hi', 1, 0, tiled=True)  140 us
    all_gather x1, waiting for transfers between devices, local(): merged = lax.all_gather(merged, 'z_hi', axis=1, tiled=True)  117 us
    another operation x36, other arithmetic, orthogonal_iteration(): lower_factor = jnp.linalg.cholesky(inner)  114 us
    another operation x24, other arithmetic, orthogonal_iteration(): jax.scipy.linalg.solve_triangular(lower_factor, image.T, lower=True)  96.3 us
    all_to_all x2, local copies, waits for them, and re-layouts, local(): rows = lax.all_to_all(own, 'z_hi', 1, 0, tiled=True)  20.1 us
  transfers between devices with their start and end apart: 15, of which 12 were waited for; matrix products, arithmetic and copies ran while one was open for 0% of the time, Pallas kernels for 0%

profile of v1, /device:TPU:33, one launch (start us, length us, event | category | flops | bytes accessed | tf_op | source)
XLA Modules:
  0.0 587.8 jit_solution(5891316470090750993)
XLA Ops:
  7.2 11.2 %all_to_all.14 = bf16[96,4,8192]{2,1,0:T(4,128)(2,1)} reshape(bf16[1,96,32768]{2,1,0:T(8,128)(2,1)} %param.4) | data formatting | bytes 12582912 | tf_op jit(solution)/shard_map/all_to_all | solution.py:117
  18.3 8.9 %copy.49 = bf16[96,4,8192]{2,0,1:T(8,128)(2,1)} copy(bf16[96,4,8192]{2,1,0:T(4,128)(2,1)} %all_to_all.14) | data formatting | bytes 12582912 | tf_op jit(solution)/shard_map/all_to_all | solution.py:117
  34.5 139.9 %all-to-all-done = bf16[96,4,8192]{2,0,1:T(8,128)(2,1)} async-done(((bf16[96,4,8192]{2,0,1:T(8,128)(2,1)}), bf16[96,4,8192]{2,0,1:T(8,128)(2,1)}, u32[]{:S(2)}, u32[]{:S(2)}) %all-to-all-start) | async-done | bytes 6291488 | tf_op jit(solution)/shard_map/all_to_all | solution.py:117
  174.4 8.8 %fusion.107 = f32[384,384]{1,0:T(8,128)S(1)} fusion(bf16[384,8192]{1,0:T(8,128)(2,1)} %bitcast.1), kind=kOutput, calls=%fused_computation.192 | convolution fusion | flops 2415919104 | bytes 6881280 | tf_op jit(solution)/shard_map/dot_general | solution.py:118
  226.2 8.8 %cholesky.194 = f32[96,96]{1,0:T(8,128)S(1)} custom-call(f32[96,96]{1,0:T(8,128)S(1)} %fusion.87), custom_call_target="Cholesky" | custom-call | tf_op jit(solution)/shard_map/jit(cholesky)/cholesky | solution.py:91
  236.3 7.4 %custom-call.16 = f32[1,96,96]{1,2,0:T(8,128)S(1)} custom-call(f32[1,96,96]{2,1,0:T(8,128)S(1)} %fusion.52), custom_call_target="InvertDiagBlocksLowerTriangular" | custom-call | tf_op jit(solution)/shard_map/jit(_solve_triangular)/triangular_solve | solution.py:92
  244.9 8.8 %cholesky.205 = f32[96,96]{1,0:T(8,128)S(1)} custom-call(f32[96,96]{1,0:T(8,128)S(1)} %fusion.85), custom_call_target="Cholesky" | custom-call | tf_op jit(solution)/shard_map/jit(cholesky)/cholesky | solution.py:91
  255.0 7.4 %custom-call.17 = f32[1,96,96]{1,2,0:T(8,128)S(1)} custom-call(f32[1,96,96]{2,1,0:T(8,128)S(1)} %fusion.53), custom_call_target="InvertDiagBlocksLowerTriangular" | custom-call | tf_op jit(solution)/shard_map/jit(_solve_triangular)/triangular_solve | solution.py:92
  263.5 8.8 %cholesky.216 = f32[96,96]{1,0:T(8,128)S(1)} custom-call(f32[96,96]{1,0:T(8,128)S(1)} %fusion.83), custom_call_target="Cholesky" | custom-call | tf_op jit(solution)/shard_map/jit(cholesky)/cholesky | solution.py:91
  273.7 7.5 %custom-call.18 = f32[1,96,96]{1,2,0:T(8,128)S(1)} custom-call(f32[1,96,96]{2,1,0:T(8,128)S(1)} %fusion.54), custom_call_target="InvertDiagBlocksLowerTriangular" | custom-call | tf_op jit(solution)/shard_map/jit(_solve_triangular)/triangular_solve | solution.py:92
  282.3 8.8 %cholesky.227 = f32[96,96]{1,0:T(8,128)S(1)} custom-call(f32[96,96]{1,0:T(8,128)S(1)} %fusion.81), custom_call_target="Cholesky" | custom-call | tf_op jit(solution)/shard_map/jit(cholesky)/cholesky | solution.py:91
  292.4 7.4 %custom-call.19 = f32[1,96,96]{1,2,0:T(8,128)S(1)} custom-call(f32[1,96,96]{2,1,0:T(8,128)S(1)} %fusion.55), custom_call_target="InvertDiagBlocksLowerTriangular" | custom-call | tf_op jit(solution)/shard_map/jit(_solve_triangular)/triangular_solve | solution.py:92
  300.9 8.8 %cholesky.238 = f32[96,96]{1,0:T(8,128)S(1)} custom-call(f32[96,96]{1,0:T(8,128)S(1)} %fusion.79), custom_call_target="Cholesky" | custom-call | tf_op jit(solution)/shard_map/jit(cholesky)/cholesky | solution.py:91
  319.5 9.0 %cholesky.249 = f32[96,96]{1,0:T(8,128)S(1)} custom-call(f32[96,96]{1,0:T(8,128)S(1)} %fusion.77), custom_call_target="Cholesky" | custom-call | tf_op jit(solution)/shard_map/jit(cholesky)/cholesky | solution.py:91
  329.8 7.4 %custom-call.21 = f32[1,96,96]{1,2,0:T(8,128)S(1)} custom-call(f32[1,96,96]{2,1,0:T(8,128)S(1)} %fusion.57), custom_call_target="InvertDiagBlocksLowerTriangular" | custom-call | tf_op jit(solution)/shard_map/jit(_solve_triangular)/triangular_solve | solution.py:92
  338.4 8.8 %cholesky.260 = f32[96,96]{1,0:T(8,128)S(1)} custom-call(f32[96,96]{1,0:T(8,128)S(1)} %fusion.75), custom_call_target="Cholesky" | custom-call | tf_op jit(solution)/shard_map/jit(cholesky)/cholesky | solution.py:91
  357.0 8.8 %cholesky.271 = f32[96,96]{1,0:T(8,128)S(1)} custom-call(f32[96,96]{1,0:T(8,128)S(1)} %fusion.73), custom_call_target="Cholesky" | custom-call | tf_op jit(solution)/shard_map/jit(cholesky)/cholesky | solution.py:91
  367.2 7.4 %custom-call.23 = f32[1,96,96]{1,2,0:T(8,128)S(1)} custom-call(f32[1,96,96]{2,1,0:T(8,128)S(1)} %fusion.59), custom_call_target="InvertDiagBlocksLowerTriangular" | custom-call | tf_op jit(solution)/shard_map/jit(_solve_triangular)/triangular_solve | solution.py:92
  376.5 9.2 %cholesky.282 = f32[96,96]{1,0:T(8,128)S(1)} custom-call(f32[96,96]{1,0:T(8,128)S(1)} %fusion.71), custom_call_target="Cholesky" | custom-call | tf_op jit(solution)/shard_map/jit(cholesky)/cholesky | solution.py:91
  387.0 7.4 %custom-call.24 = f32[1,96,96]{1,2,0:T(8,128)S(1)} custom-call(f32[1,96,96]{2,1,0:T(8,128)S(1)} %fusion.60), custom_call_target="InvertDiagBlocksLowerTriangular" | custom-call | tf_op jit(solution)/shard_map/jit(_solve_triangular)/triangular_solve | solution.py:92
  395.5 8.8 %cholesky.293 = f32[96,96]{1,0:T(8,128)S(1)} custom-call(f32[96,96]{1,0:T(8,128)S(1)} %fusion.69), custom_call_target="Cholesky" | custom-call | tf_op jit(solution)/shard_map/jit(cholesky)/cholesky | solution.py:91
  414.2 8.8 %cholesky.304 = f32[96,96]{1,0:T(8,128)S(1)} custom-call(f32[96,96]{1,0:T(8,128)S(1)} %fusion.67), custom_call_target="Cholesky" | custom-call | tf_op jit(solution)/shard_map/jit(cholesky)/cholesky | solution.py:91
  433.0 8.8 %cholesky.315 = f32[96,96]{1,0:T(8,128)S(1)} custom-call(f32[96,96]{1,0:T(8,128)S(1)} %fusion.65), custom_call_target="Cholesky" | custom-call | tf_op jit(solution)/shard_map/jit(cholesky)/cholesky | solution.py:91
  457.6 117.3 %all-gather.2.cloned.1.call-done = bf16[96,32768]{1,0:T(8,128)(2,1)} async-done(((bf16[96,8192]{1,0:T(8,128)(2,1)}), bf16[96,32768]{1,0:T(8,128)(2,1)}) %all-gather.2.cloned.1.call-update) | async-done | bytes 6291472 | tf_op jit(solution)/shard_map/all_gather | solution.py:123
  (158 shorter events, 129.2 us)
Async XLA Ops:
  27.2 147.2 %all-to-all-start = ((bf16[96,4,8192]{2,0,1:T(8,128)(2,1)}), bf16[96,4,8192]{2,0,1:T(8,128)(2,1)}, u32[]{:S(2)}, u32[]{:S(2)}) async-start(bf16[96,4,8192]{2,0,1:T(8,128)(2,1)} %copy.49), calls=%async_computation | async-start | bytes 12582912 | tf_op jit(solution)/shard_map/all_to_all | solution.py:117
  34.5 540.3 %all-gather.2.cloned.1.call-start = ((), (), s32[]{:S(2)}) async-start(), calls=%async_computation.1 | async-start | bytes 7864320 | tf_op jit(solution)/shard_map/all_gather | solution.py:123
  183.3 2.9 collective-permute-start
  186.3 4.1 collective-permute-start.1
  190.5 4.3 collective-permute-start.2
  191.7 3.0 collective-permute-start.4
  193.2 4.2 collective-permute-start.3
  197.4 3.7 collective-permute-start.7
  198.2 6.6 %collective-permute-start.6 = (f32[48,128]{1,0:T(8,128)S(1)}, f32[48,128]{1,0:T(8,128)S(1)}, u32[]{:S(2)}, u32[]{:S(2)}) collective-permute-start(f32[48,128]{1,0:T(8,128)S(1)} %fusion.96), channel_id=1, source_target_pairs={{0,32},{16,48},{32,0},{48,16},{1,33},{17,49},{33,1},{49,17},{2,34}... | collective-permute-start | bytes 73736 | tf_op jit(solution)/shard_map/ppermute | solution.py:16
  201.1 4.8 collective-permute-start.5
  205.9 3.3 collective-permute-start.10
  207.7 4.2 collective-permute-start.9
  208.2 4.0 collective-permute-start.8
  212.7 3.8 collective-permute-start.11
  216.6 8.4 %collective-permute-start.12 = (f32[384,128]{1,0:T(8,128)S(1)}, f32[384,128]{1,0:T(8,128)S(1)}, u32[]{:S(2)}, u32[]{:S(2)}) collective-permute-start(f32[384,128]{1,0:T(8,128)S(1)} %pad_maximum_fusion.10), channel_id=1, source_target_pairs={{0,1},{1,0},{2,3},{3,2},{4,5},{5,4},{6,7},{7,6},{8,9},{9,8},{10,11... | collective-permute-start | bytes 589832 | tf_op jit(solution)/shard_map/ppermute | solution.py:11
Sparse Core Ops, SparseCore 0:
  456.5 118.3 all-gather.1
